TPU v7x, 512 devices: a whole 4x8x8 slice. The times are simulated.
512 devices in a mesh: band: 16 (over x, z_hi, core), ga: 32 (over y, z_lo).
Axes of the slice: x: 4, y: 8, z: 8 (z_hi: 2, z_lo: 4; z = z_hi * 4 + z_lo), core: 2. Of those that a mesh axis runs over, the one named last changes fastest.
Arguments:
- psi_block: bfloat16 [16, 2048, 256], P('band', 'ga'), may hold values from -6 to 6
- potential: bfloat16 [256, 256, 256], P('ga'), may hold values from -2.5 to 1.5
- resident: bfloat16 [256, 2048, 256], P('band', 'ga'), may hold values from -0.013671875 to 0.013671875
- stick_cols: int32 [2048], P('ga'), may hold values from 0 to 65535, as said below
- stick_counts: int32 [2048], P('ga'), may hold values from 1 to 129, as said below
- plane_order: int32 [256], replicated, may hold values from 0 to 255, each once
Outputs:
- applied: bfloat16 [16, 2048, 256], P('band', 'ga')
- intersection: float32 [256, 16], P('band')
Inputs may be any that keep to these rules, and one draw needn't show every extreme that they name: `stick_cols`: distinct columns kx * 256 + ky whose signed frequencies satisfy f(kx)^2 + f(ky)^2 <= 64^2; column 0, column (64) * 256 and column 65535 are always present. `stick_counts`: 2 h + 1, with h the largest integer such that h^2 + f(kx)^2 + f(ky)^2 <= 64^2 for the stick's column. `plane_order`: A permutation of the z-planes.
All inputs are finite; a program needn't handle non-finite values.
Results may differ from a plain program's by a relative error of at most 0.0072.
Values may be sent and summed in bfloat16 or wider, within the bound.
A program may use at most 64 MiB of HBM per device.

v0:
```python
import math

import jax
import jax.numpy as jnp
from jax import lax
from jax.sharding import PartitionSpec as P


def hartley_table(row_index, col_index, grid_size):
    product = row_index[:, None] * col_index[None, :] % grid_size
    angle = product.astype(jnp.float32) * (2.0 * math.pi / grid_size)
    return ((jnp.cos(angle) + jnp.sin(angle)) * (1.0 / math.sqrt(grid_size))).astype(jnp.bfloat16)


def body(psi_block, potential, resident, stick_cols, stick_counts, plane_order):
    grid_size = psi_block.shape[2]
    planes_here = potential.shape[0]
    frequency = jnp.arange(grid_size, dtype=jnp.int32)
    grid_table = hartley_table(frequency, frequency, grid_size)
    z_table = hartley_table(frequency, plane_order, grid_size)
    signed_freq = jnp.where(frequency < grid_size // 2, frequency, frequency - grid_size)
    sphere = 2 * jnp.abs(signed_freq)[None, :] + 1 <= stick_counts[:, None]
    masked = jnp.where(sphere[None], psi_block, jnp.zeros((), jnp.bfloat16))
    zreal = jnp.einsum("kp,bsk->bps", z_table, masked, preferred_element_type=jnp.float32).astype(
        jnp.bfloat16
    )
    all_columns = lax.all_gather(stick_cols, "ga", axis=0, tiled=True)
    potential_wide = potential.astype(jnp.float32)
    item_rows = lax.all_to_all(zreal, "ga", split_axis=1, concat_axis=2, tiled=True)
    item_count = item_rows.shape[0]
    spread = jnp.zeros((item_count, planes_here, grid_size * grid_size), jnp.bfloat16)
    spread = (
        spread.at[:, :, all_columns]
        .set(item_rows)
        .reshape(item_count, planes_here, grid_size, grid_size)
    )
    halfway = jnp.einsum(
        "kx,bpkq->bpxq", grid_table, spread, preferred_element_type=jnp.float32
    ).astype(jnp.bfloat16)
    field = jnp.einsum("bpxq,qy->bpxy", halfway, grid_table, preferred_element_type=jnp.float32)
    weighted = (potential_wide[None] * field).astype(jnp.bfloat16)
    backward = jnp.einsum(
        "bpxy,yq->bpxq", weighted, grid_table, preferred_element_type=jnp.float32
    ).astype(jnp.bfloat16)
    spectrum = jnp.einsum(
        "xk,bpxq->bpkq", grid_table, backward, preferred_element_type=jnp.float32
    ).astype(jnp.bfloat16)
    picked = spectrum.reshape(item_count, planes_here, grid_size * grid_size)[:, :, all_columns]
    returned = lax.all_to_all(picked, "ga", split_axis=2, concat_axis=1, tiled=True)
    result = jnp.einsum("bps,kp->bsk", returned, z_table, preferred_element_type=jnp.float32)
    applied = jnp.where(sphere[None], result, jnp.float32(0.0)).astype(jnp.bfloat16)
    product_part = jnp.einsum(
        "rsk,bsk->rb",
        resident,
        lax.all_gather(applied, "band", axis=0, tiled=True),
        preferred_element_type=jnp.float32,
    )
    intersection = lax.psum(product_part, "ga")
    return (applied, intersection)


def solution(mesh):
    in_specs = (
        P("band", "ga", None),
        P("ga", None, None),
        P("band", "ga", None),
        P("ga"),
        P("ga"),
        P(),
    )
    out_specs = (P("band", "ga", None), P("band", None))
    return jax.shard_map(body, mesh=mesh, in_specs=in_specs, out_specs=out_specs, check_vma=False)
```

profile of v0, /device:TPU:6, one launch (start us, length us, event | category | flops | bytes accessed | tf_op | source)
XLA Modules:
  0.0 258.0 jit_solution(7189995870175544483)
XLA Ops:
  0.6 0.0 copy-start
  0.7 2.0 fusion.5
  2.7 0.1 copy.46
  2.8 0.5 broadcast.137
  3.3 1.0 reduce
  4.3 0.7 reshape.135
  5.0 12.9 %all-to-all-start = ((bf16[32,2,256]{2,1,0:T(2,128)(2,1)}), bf16[32,2,256]{2,1,0:T(2,128)(2,1)S(1)}, u32[]{:S(2)}, u32[]{:S(2)}) async-start(bf16[32,2,256]{2,1,0:T(2,128)(2,1)} %reshape.135), calls=%async_computation | async-start | bytes 65536 | tf_op jit(solution)/shard_map/all_to_all | solution.py:29
  17.9 1.3 dynamic-slice
  19.9 0.9 dynamic-update-slice
  20.7 20.3 %all-reduce = s32[2048]{0:T(1024)S(1)} all-reduce(s32[2048]{0:T(1024)S(1)} %dynamic-update-slice), channel_id=1, replica_groups=mesh['band'=16,'ga'=32] {'ga'}, use_global_device_ids=true, to_apply=%add | all-reduce | flops 2048 | bytes 16384
  41.1 0.1 reshape.136
  41.2 0.1 reshape.111
  41.3 0.3 copy.48
  41.7 15.1 %scatter_custom_fusion = bf16[8,65536]{0,1:T(8,128)(2,1)} fusion(s32[2048]{0:T(1024)S(1)} %get-tuple-element.13, bf16[2048,8]{1,0:T(8,128)(2,1)S(1)} %copy.48, bf16[]{:T(256)} %constant.33.clone.1), kind=kCustom, calls=%fused_computation.2 | custom fusion | bytes 1048578 | tf_op jit(solution)/shard_map/scatter | solution.py:34
  56.8 15.9 %copy.49 = bf16[8,256,256]{1,2,0:T(8,128)(2,1)S(1)} copy(bf16[8,256,256]{0,2,1:T(8,128)(2,1)} %bitcast.58) | data formatting | bytes 2097152 | tf_op jit(solution)/shard_map/reshape.4
  72.7 0.0 copy-start.3
  72.7 3.2 %multiply_convert_fusion = bf16[8,256,256]{2,1,0:T(8,128)(2,1)} fusion(bf16[8,256,256]{2,1,0:T(8,128)(2,1)S(1)} %copy-done.2, bf16[8,256,256]{1,2,0:T(8,128)(2,1)S(1)} %copy.49), kind=kOutput, calls=%fused_computation.4 | convolution fusion | flops 541196288 | bytes 3145728 | tf_op jit(solution)/shard_map/bpxq,qy->bpxy/dot_general | solution.py:40
  75.9 3.4 %fusion.3 = bf16[1,8,256,256]{2,3,1,0:T(8,128)(2,1)S(1)} fusion(bf16[8,256,256]{2,1,0:T(8,128)(2,1)} %multiply_convert_fusion), kind=kOutput, calls=%fused_computation.9 | convolution fusion | flops 540147712 | bytes 2097152 | tf_op jit(solution)/shard_map/xk,bpxq->bpkq/dot_general | solution.py:45
  79.3 12.4 %copy.62 = bf16[1,8,256,256]{1,3,2,0:T(8,128)(2,1)} copy(bf16[1,8,256,256]{2,3,1,0:T(8,128)(2,1)S(1)} %fusion.3) | data formatting | bytes 2097152 | tf_op jit(solution)/shard_map/reshape | solution.py:48
  91.7 13.5 %gather_fusion = bf16[2048,8]{1,0:T(8,128)(2,1)S(1)} fusion(bf16[8,65536]{0,1:T(8,128)(2,1)} %bitcast.59, s32[2048]{0:T(1024)S(1)} %get-tuple-element.12), kind=kCustom, calls=%fused_computation | custom fusion | bytes 73728 | tf_op jit(solution)/shard_map/gather | solution.py:48
  105.2 8.4 %copy.76 = bf16[1,8,2048]{1,0,2:T(2,128)(2,1)S(1)} copy(bf16[1,8,2048]{1,2,0:T(8,128)(2,1)S(1)} %bitcast.62) | data formatting | bytes 65536 | tf_op jit(solution)/shard_map/gather | solution.py:48
  113.6 11.5 %reduce.1 = bf16[2048,8]{1,0:T(8,128)(2,1)S(1)} reduce(bf16[2048,1,8]{2,1,0:T(2,128)(2,1)S(1)} %bitcast.60, bf16[]{:T(256)} %broadcast.137), dimensions={1}, to_apply=%bitcast.56.reduce_sub_computation | reduce | bytes 65538
  125.1 0.6 reshape.137
  125.7 15.9 %all_to_all.33 = bf16[32,2,256]{2,1,0:T(2,128)(2,1)S(1)} all-to-all(bf16[32,2,256]{2,1,0:T(2,128)(2,1)S(1)} %reshape.137), channel_id=1, replica_groups=mesh['band'=16,'ga'=32] {'ga'}, dimensions={0} | all-to-all | bytes 65536 | tf_op jit(solution)/shard_map/all_to_all | solution.py:49
  141.6 1.4 reshape.138
  143.0 0.5 copy.55
  143.5 0.1 all_to_all.29
  143.6 1.2 fusion.4
  144.8 32.4 %all-gather = bf16[1024,256]{1,0:T(8,128)(2,1)S(1)} all-gather(bf16[64,256]{1,0:T(8,128)(2,1)S(1)} %fusion.4), channel_id=2, replica_groups=mesh['band'=16,'ga'=32] {'band'}, dimensions={0}, use_global_device_ids=true | all-gather | bytes 557056 | tf_op jit(solution)/shard_map/all_gather | solution.py:55
  177.2 0.7 convolution_bitcast_fusion
  177.9 79.4 %psum.7 = f32[16,16]{0,1:T(8,128)S(1)} all-reduce(f32[16,16]{0,1:T(8,128)S(1)} %convolution_bitcast_fusion), channel_id=1, replica_groups=mesh['band'=16,'ga'=32] {'ga'}, use_global_device_ids=true, to_apply=%region_1.2 | all-reduce | flops 256 | bytes 2048 | tf_op jit(solution)/shard_map/psum | solution.py:58
  257.3 0.7 copy.59
  (14 shorter events, 0.1 us)
Async XLA Ops:
  0.6 176.6 %copy-start = (bf16[16,64,256]{2,1,0:T(8,128)(2,1)S(1)}, bf16[16,64,256]{2,1,0:T(8,128)(2,1)}, u32[]{:S(2)}) copy-start(bf16[16,64,256]{2,1,0:T(8,128)(2,1)} %param.8) | copy-start | bytes 1572868
  5.0 36.0 %all-to-all-start = ((bf16[32,2,256]{2,1,0:T(2,128)(2,1)}), bf16[32,2,256]{2,1,0:T(2,128)(2,1)S(1)}, u32[]{:S(2)}, u32[]{:S(2)}) async-start(bf16[32,2,256]{2,1,0:T(2,128)(2,1)} %reshape.135), calls=%async_computation | async-start | bytes 65536 | tf_op jit(solution)/shard_map/all_to_all | solution.py:29
  41.7 31.0 %copy-start.2 = (bf16[8,256,256]{2,1,0:T(8,128)(2,1)S(1)}, bf16[8,256,256]{2,1,0:T(8,128)(2,1)}, u32[]{:S(2)}) copy-start(bf16[8,256,256]{2,1,0:T(8,128)(2,1)} %param.7) | copy-start | bytes 3145732
  72.7 70.9 %copy-start.3 = (s32[256]{0:T(256)S(1)}, s32[256]{0:T(256)}, u32[]{:S(2)}) copy-start(s32[256]{0:T(256)} %param.11) | copy-start | bytes 3076
  72.7 70.9 %copy-start.4 = (s32[64]{0:T(128)S(1)}, s32[64]{0:T(128)}, u32[]{:S(2)}) copy-start(s32[64]{0:T(128)} %param.10) | copy-start | bytes 772
  144.8 113.2 %copy-start.1 = (bf16[64,256]{1,0:T(8,128)(2,1)}, bf16[64,256]{1,0:T(8,128)(2,1)S(1)}, u32[]{:S(2)}) copy-start(bf16[64,256]{1,0:T(8,128)(2,1)S(1)} %fusion.4) | copy-start | bytes 98308
where the time goes:
time: 259 us; the launch traced here: 258 us
  blocking collectives  148 us (57%)
  local copies, waits for them, and re-layouts  72.6 us (28%)
  starting transfers between devices  12.9 us (5%)
  other arithmetic  12.4 us (5%)
  matrix products  10.5 us (4%)
    psum x1, blocking collectives, body(): intersection = lax.psum(product_part, 'ga')  79.4 us
    all_gather x1, blocking collectives, body(): lax.all_gather(applied, 'band', axis=0, tiled=True)  32.4 us
    gather x2, local copies, waits for them, and re-layouts, body(): spectrum.reshape(item_count, planes_here, grid_size * grid_size)  21.9 us
    unnamed x1, blocking collectives  20.3 us
    all_to_all x1, blocking collectives, body(): lax.all_to_all(picked, 'ga', split_axis=2, concat_axis=1, tiled=True)  15.9 us
    another operation x1, local copies, waits for them, and re-layouts  15.9 us
    scatter x1, local copies, waits for them, and re-layouts, body(): spread = spread.at[:, :, all_columns].set(item_rows).reshape(item_count,...  15.1 us
    all_to_all x1, starting transfers between devices, body(): lax.all_to_all(zreal, 'ga', split_axis=1, concat_axis=2, tiled=True)  12.9 us
  transfers between devices with their start and end apart: 1, of which 0 were waited for; matrix products, arithmetic and copies ran while one was open for 1% of the time, Pallas kernels for 0%

commit v1 on v0

v1 whole, which is shorter than its diff:
```python
import functools

import jax
import jax.numpy as jnp
import numpy as np
from jax import lax
from jax.experimental import pallas as pl
from jax.experimental.pallas import tpu as pltpu
from jax.sharding import PartitionSpec as P

MESH = pl.DeviceIdType.MESH
GRID = 256
RADIUS = 64
ROWS = 144
TILE = 256
F32 = jnp.float32
BF16 = jnp.bfloat16
EXACT = lax.Precision.HIGHEST


def hartley_tables():
    k = np.arange(GRID)
    angle = (k[:, None] * k[None, :] % GRID).astype(np.float32) * np.float32(2.0 * np.pi / GRID)
    table = ((np.cos(angle) + np.sin(angle)) * np.float32(1.0 / np.sqrt(GRID))).astype(BF16)
    disc = np.zeros((ROWS, GRID), BF16)
    disc[: 2 * RADIUS + 1] = table[np.arange(-RADIUS, RADIUS + 1) % GRID]
    return table, disc, np.ascontiguousarray(disc.T)


def iota(shape, axis):
    return lax.broadcasted_iota(jnp.int32, shape, axis)


def dot(a, b, ca, cb, precision=None):
    return lax.dot_general(
        a, b, (((ca,), (cb,)), ((), ())), precision=precision, preferred_element_type=F32
    )


def kernel(
    n_band,
    n_ga,
    psi_ref,
    pot_ref,
    res_ref,
    cols_ref,
    counts_ref,
    order_ref,
    table_ref,
    disc_ref,
    disc_t_ref,
    applied_ref,
    inter_ref,
    psi_v,
    pot_v,
    res_v,
    table_v,
    disc_v,
    disc_t_v,
    out_v,
    ztab_v,
    cols_send,
    cols_recv,
    z_send,
    z_recv,
    pick_send,
    pick_recv,
    onehot_x,
    table_y,
    half_acc,
    half_v,
    back_v,
    gather,
    red_send,
    red_recv,
    load_sem,
    send_sem,
    recv_sem,
    out_sem,
):
    me_b, me_g = lax.axis_index("band"), lax.axis_index("ga")
    sticks, planes = psi_ref.shape[0], pot_ref.shape[0]
    tiles = n_ga * sticks // TILE
    parity = lax.rem(me_g, 2)
    pairs = n_ga // 2

    loads = [
        pltpu.make_async_copy(src, dst, load_sem.at[i])
        for i, (src, dst) in enumerate(
            (
                (psi_ref, psi_v),
                (table_ref, table_v),
                (disc_ref, disc_v),
                (disc_t_ref, disc_t_v),
                (pot_ref, pot_v),
                (res_ref, res_v),
            )
        )
    ]
    for load in loads:
        load.start()

    barrier = pltpu.get_barrier_semaphore()

    @pl.loop(1, n_ga)
    def _(d):
        to = lax.rem(me_g + d, n_ga)
        pl.semaphore_signal(barrier, inc=1, device_id={"ga": to}, device_id_type=MESH)

    @pl.loop(1, n_band)
    def _(d):
        to = lax.rem(me_b + d, n_band)
        pl.semaphore_signal(barrier, inc=1, device_id={"band": to}, device_id_type=MESH)

    def send_ga(src, dst, phase, to):
        pltpu.make_async_remote_copy(
            src_ref=src,
            dst_ref=dst,
            send_sem=send_sem.at[phase],
            recv_sem=recv_sem.at[phase],
            device_id={"ga": to},
            device_id_type=MESH,
        ).start()

    def wait_bytes(ref, sem):
        pltpu.make_async_copy(ref, ref, sem).wait()

    counts = jnp.where(
        iota((sticks, sticks), 0) == iota((sticks, sticks), 1), counts_ref[...].astype(F32), 0.0
    ).sum(axis=1, keepdims=True)
    k = iota((sticks, GRID), 1)
    freq = jnp.where(k < GRID // 2, k, GRID - k)
    sphere = (2 * freq + 1).astype(F32) <= counts

    lane_half = iota((1, 2 * sticks), 1) // sticks
    own_half = lane_half == parity
    cols = cols_ref[...]
    cols_send[...] = jnp.where(own_half, jnp.concatenate([cols, cols], axis=1), 0)

    for load in loads[:4]:
        load.wait()
    order_pick = (iota((GRID, n_ga * planes), 0) == order_ref[...]).astype(F32).astype(BF16)
    ztab = dot(order_pick, table_v[...], 0, 0).astype(BF16)
    ztab_v[...] = ztab
    masked = jnp.where(sphere, psi_v[...].astype(F32), 0.0)
    two = jnp.concatenate(
        [jnp.where(parity == 0, masked, 0.0), jnp.where(parity == 1, masked, 0.0)], axis=0
    ).astype(BF16)
    zreal = dot(ztab, two, 1, 1).astype(BF16).astype(F32)
    z_send[...] = zreal.reshape(n_ga, planes, 2 * sticks)
    cols_recv[me_g] = cols_send[...]
    z_recv[me_g] = z_send[me_g]

    pl.semaphore_wait(barrier, n_ga + n_band - 2)

    @pl.loop(1, n_ga)
    def _(d):
        to = lax.rem(me_g + d, n_ga)
        send_ga(cols_send, cols_recv.at[me_g], 0, to)

    @pl.loop(1, n_ga)
    def _(d):
        to = lax.rem(me_g + d, n_ga)
        send_ga(z_send.at[to], z_recv.at[me_g], 1, to)

    wait_bytes(cols_recv.at[pl.ds(0, n_ga - 1)], recv_sem.at[0])

    @pl.loop(0, tiles)
    def _(t):
        col = jnp.concatenate(
            [cols_recv[4 * t] + cols_recv[4 * t + 1], cols_recv[4 * t + 2] + cols_recv[4 * t + 3]],
            axis=1,
        )
        kx, ky = lax.shift_right_logical(col, 8), col & (GRID - 1)
        row = jnp.where(kx < GRID // 2, kx + RADIUS, kx + RADIUS - GRID)
        onehot_x[t] = (iota((ROWS, TILE), 0) == row).astype(F32).astype(BF16)
        onehot_y = (iota((GRID, TILE), 0) == ky).astype(F32).astype(BF16)
        table_y[t] = dot(table_v[...], onehot_y, 1, 0).astype(BF16)

    wait_bytes(z_recv.at[pl.ds(0, n_ga - 1)], recv_sem.at[1])
    half_acc[...] = jnp.zeros_like(half_acc)

    @pl.loop(0, tiles)
    def _(t):
        z = jnp.concatenate(
            [z_recv[4 * t] + z_recv[4 * t + 1], z_recv[4 * t + 2] + z_recv[4 * t + 3]], axis=1
        )
        pick = onehot_x[t].reshape(ROWS // 16, 16, TILE)
        spread = jnp.concatenate(
            [
                (pick * jnp.broadcast_to(z[p : p + 1], (16, TILE)).astype(BF16)[None]).reshape(
                    ROWS, TILE
                )
                for p in range(planes)
            ],
            axis=0,
        )
        half_acc[...] += dot(spread, table_y[t], 1, 1)

    half_v[...] = half_acc[...].astype(BF16).reshape(planes, ROWS, GRID)
    loads[4].wait()

    @pl.loop(0, planes)
    def _(p):
        field = dot(disc_t_v[...], half_v[p], 1, 0)
        weighted = (pot_v[p].astype(F32) * field).astype(BF16)
        back_v[p] = dot(disc_v[...], weighted, 1, 0).astype(BF16)

    @pl.loop(0, tiles)
    def _(step):
        t = lax.rem(step + me_g // 4, tiles)
        spectrum = dot(back_v[...].reshape(planes * ROWS, GRID), table_y[t], 1, 0)
        picked = (spectrum.reshape(planes, ROWS, TILE) * onehot_x[t].astype(F32)[None]).sum(axis=1)
        picked = picked.astype(BF16).astype(F32)
        pick_send[2 * t] = picked[:, : 2 * sticks]
        pick_send[2 * t + 1] = picked[:, 2 * sticks :]
        for i in range(4):
            to = 4 * t + i

            @pl.when(to != me_g)
            def _():
                send_ga(pick_send.at[2 * t + i // 2], pick_recv.at[me_g], 2, to)

            @pl.when(to == me_g)
            def _():
                pick_recv[me_g] = pick_send[2 * t + i // 2]

    wait_bytes(pick_recv.at[pl.ds(0, n_ga - 1)], recv_sem.at[2])
    returned = jnp.where(own_half, pick_recv[...].reshape(n_ga * planes, 2 * sticks), 0.0)
    result = dot(returned.astype(BF16), ztab_v[...], 0, 0)
    result = result[:sticks] + result[sticks:]
    applied = jnp.where(sphere, result, 0.0).astype(BF16)
    out_v[...] = applied
    gather[me_b] = applied
    store = pltpu.make_async_copy(out_v, applied_ref, out_sem.at[0])
    store.start()

    @pl.loop(1, n_band)
    def _(d):
        to = lax.rem(me_b + d, n_band)
        pltpu.make_async_remote_copy(
            src_ref=out_v,
            dst_ref=gather.at[me_b],
            send_sem=send_sem.at[3],
            recv_sem=recv_sem.at[3],
            device_id={"band": to},
            device_id_type=MESH,
        ).start()

    loads[5].wait()
    wait_bytes(gather.at[pl.ds(0, n_band - 1)], recv_sem.at[3])
    n_res = res_v.shape[0]
    prod = jnp.zeros((n_res * 16, n_band * 16), F32)
    for g in range(sticks // 16):
        left = res_v[:, 16 * g : 16 * g + 16, :].reshape(n_res * 16, GRID)
        right = gather[:, 16 * g : 16 * g + 16, :].reshape(n_band * 16, GRID)
        prod += dot(left, right, 1, 1)
    same = iota(prod.shape, 0) % 16 == iota(prod.shape, 1) % 16
    summed = jnp.where(same, prod, 0.0).reshape(n_res, 16, n_band * 16).sum(axis=1)
    fold = (iota((n_band * 16, 128), 0) // 16 == iota((n_band * 16, 128), 1) % 16).astype(F32)
    part = dot(summed, fold, 1, 0, EXACT)
    part = jnp.where(iota(part.shape, 1) // 16 == iota(part.shape, 0) % 8, part, 0.0)
    red_send[...] = part.reshape(n_res // 8, 8, 128).sum(axis=1)
    red_recv[me_g] = red_send[...]

    @pl.loop(1, n_ga)
    def _(d):
        to = lax.rem(me_g + d, n_ga)
        send_ga(red_send, red_recv.at[me_g], 4, to)

    wait_bytes(red_recv.at[pl.ds(0, n_ga - 1)], recv_sem.at[4])
    inter_ref[...] = red_recv[...].sum(axis=0)

    store.wait()
    wait_bytes(cols_recv.at[pl.ds(0, n_ga - 1)], send_sem.at[0])
    wait_bytes(z_recv.at[pl.ds(0, n_ga - 1)], send_sem.at[1])
    wait_bytes(pick_recv.at[pl.ds(0, n_ga - 1)], send_sem.at[2])
    wait_bytes(gather.at[pl.ds(0, n_band - 1)], send_sem.at[3])
    wait_bytes(red_recv.at[pl.ds(0, n_ga - 1)], send_sem.at[4])


def body(n_band, n_ga, psi_block, potential, resident, stick_cols, stick_counts, plane_order):
    sticks, planes, n_res = psi_block.shape[1], potential.shape[0], resident.shape[0]
    tiles = n_ga * sticks // TILE
    table, disc, disc_t = hartley_tables()
    any_space = pl.BlockSpec(memory_space=pl.ANY)
    vmem = pl.BlockSpec(memory_space=pltpu.VMEM)
    applied, inter = pl.pallas_call(
        functools.partial(kernel, n_band, n_ga),
        out_shape=(
            jax.ShapeDtypeStruct((sticks, GRID), BF16),
            jax.ShapeDtypeStruct((n_res // 8, 128), F32),
        ),
        in_specs=[any_space] * 3 + [vmem] * 3 + [any_space] * 3,
        out_specs=(any_space, vmem),
        scratch_shapes=[
            pltpu.VMEM((sticks, GRID), BF16),
            pltpu.VMEM(potential.shape, BF16),
            pltpu.VMEM(resident.shape, BF16),
            pltpu.VMEM(table.shape, BF16),
            pltpu.VMEM(disc.shape, BF16),
            pltpu.VMEM(disc_t.shape, BF16),
            pltpu.VMEM((sticks, GRID), BF16),
            pltpu.VMEM((n_ga * planes, GRID), BF16),
            pltpu.VMEM((1, 2 * sticks), jnp.int32),
            pltpu.VMEM((n_ga, 1, 2 * sticks), jnp.int32),
            pltpu.VMEM((n_ga, planes, 2 * sticks), F32),
            pltpu.VMEM((n_ga, planes, 2 * sticks), F32),
            pltpu.VMEM((n_ga // 2, planes, 2 * sticks), F32),
            pltpu.VMEM((n_ga, planes, 2 * sticks), F32),
            pltpu.VMEM((tiles, ROWS, TILE), BF16),
            pltpu.VMEM((tiles, GRID, TILE), BF16),
            pltpu.VMEM((planes * ROWS, GRID), F32),
            pltpu.VMEM((planes, ROWS, GRID), BF16),
            pltpu.VMEM((planes, ROWS, GRID), BF16),
            pltpu.VMEM((n_band, sticks, GRID), BF16),
            pltpu.VMEM((n_res // 8, 128), F32),
            pltpu.VMEM((n_ga, n_res // 8, 128), F32),
            pltpu.SemaphoreType.DMA((6,)),
            pltpu.SemaphoreType.DMA((5,)),
            pltpu.SemaphoreType.DMA((5,)),
            pltpu.SemaphoreType.DMA((1,)),
        ],
        compiler_params=pltpu.CompilerParams(
            collective_id=0, has_side_effects=True, vmem_limit_bytes=40 * 2**20
        ),
    )(
        psi_block[0],
        potential,
        resident,
        stick_cols[None],
        stick_counts[None],
        plane_order[None],
        table,
        disc,
        disc_t,
    )
    return applied[None], inter.reshape(n_res, 16)[:, :n_band]


def solution(mesh):
    in_specs = (
        P("band", "ga", None),
        P("ga", None, None),
        P("band", "ga", None),
        P("ga"),
        P("ga"),
        P(),
    )
    out_specs = (P("band", "ga", None), P("band", None))
    step = functools.partial(body, mesh.shape["band"], mesh.shape["ga"])
    return jax.shard_map(step, mesh=mesh, in_specs=in_specs, out_specs=out_specs, check_vma=False)
```

time: 259 us -> 66 us (0.25)
  the two profiles are of different devices: /device:TPU:6 before, /device:TPU:1 now
where the time goes in v1:
time: 66 us; the launch traced here: 65.7 us
  Pallas kernels  57.3 us (87%)
  local copies, waits for them, and re-layouts  7.68 us (12%)
  between operations  0.67 us (1%)
    pallas_call x1, Pallas kernels, body(): pl.pallas_call(functools.partial(kernel, n_band, n_ga), out_shape=(jax.Sh...  57.3 us
    unnamed x19, local copies, waits for them, and re-layouts  7 us

profile of v1, /device:TPU:1, one launch (start us, length us, event | category | flops | bytes accessed | tf_op | source)
XLA Modules:
  0.0 65.7 jit_solution(4282372969604630953)
XLA Ops:
  0.6 0.0 copy-start.8
  0.6 0.0 copy-start.6
  0.7 0.0 copy-start.7
  0.7 0.6 copy-done.8
  1.3 0.0 copy-done.6
  1.3 0.0 copy-done.7
  1.3 0.0 copy-start
  1.3 1.2 %copy-done = bf16[8,256,256]{2,1,0:T(8,128)(2,1)S(1)} copy-done((bf16[8,256,256]{2,1,0:T(8,128)(2,1)S(1)}, bf16[8,256,256]{2,1,0:T(8,128)(2,1)}, u32[]{:S(2)}) %copy-start) | copy-done | bytes 1048600
  2.6 0.0 copy-start.1
  2.6 1.0 %copy-done.1 = bf16[16,64,256]{2,1,0:T(8,128)(2,1)S(1)} copy-done((bf16[16,64,256]{2,1,0:T(8,128)(2,1)S(1)}, bf16[16,64,256]{2,1,0:T(8,128)(2,1)}, u32[]{:S(2)}) %copy-start.1) | copy-done | bytes 524312
  3.6 0.0 copy-start.2
  3.6 0.9 %copy-done.2 = bf16[256,144]{1,0:T(8,128)(2,1)S(1)} copy-done((bf16[256,144]{1,0:T(8,128)(2,1)S(1)}, bf16[256,144]{1,0:T(8,128)(2,1)}, u32[]{:S(2)}) %copy-start.2) | copy-done | bytes 73752
  4.5 0.0 copy-start.3
  4.5 0.9 %copy-done.3 = bf16[256,256]{1,0:T(8,128)(2,1)S(1)} copy-done((bf16[256,256]{1,0:T(8,128)(2,1)S(1)}, bf16[256,256]{1,0:T(8,128)(2,1)}, u32[]{:S(2)}) %copy-start.3) | copy-done | bytes 131096
  5.4 0.0 copy-start.4
  5.4 0.9 %copy-done.4 = bf16[144,256]{1,0:T(8,128)(2,1)S(1)} copy-done((bf16[144,256]{1,0:T(8,128)(2,1)S(1)}, bf16[144,256]{1,0:T(8,128)(2,1)}, u32[]{:S(2)}) %copy-start.4) | copy-done | bytes 73752
  6.3 0.0 copy-start.5
  6.3 0.8 %copy-done.5 = bf16[1,64,256]{2,1,0:T(8,128)(2,1)S(1)} copy-done((bf16[1,64,256]{2,1,0:T(8,128)(2,1)S(1)}, bf16[1,64,256]{2,1,0:T(8,128)(2,1)}, u32[]{:S(2)}) %copy-start.5) | copy-done | bytes 32792
  7.1 57.3 %shard_map.104 = (bf16[64,256]{1,0:T(8,128)(2,1)S(1)}, f32[2,128]{1,0:T(2,128)S(1)}) custom-call(bf16[64,256]{1,0:T(8,128)(2,1)S(1)} %bitcast.5, bf16[8,256,256]{2,1,0:T(8,128)(2,1)S(1)} %copy-done, bf16[16,64,256]{2,1,0:T(8,128)(2,1)S(1)} %copy-done.1, s32[1,64]{1,0:T(1,128)S(1)} %bitcast.8, s32[1,64]{1,0:T(1,128)S(1)} %bitcast.9, s32[1,256]{1,0:T(1,128)S(1)} %bitcast.7, ...), custom_call_target="tpu_custom_call" | custom-call | tf_op jit(solution)/shard_map/pallas_call | solution.py:288
  64.4 0.7 %reshape.7 = f32[16,16]{1,0:T(8,128)} reshape(f32[2,128]{1,0:T(2,128)S(1)} %get-tuple-element.5) | data formatting | bytes 2048 | tf_op jit(solution)/shard_map/reshape | solution.py:338
  65.1 0.6 copy.12
Async XLA Ops:
  0.6 0.7 copy-start.8
  0.6 0.7 %copy-start.6 = (s32[256]{0:T(256)S(1)}, s32[256]{0:T(256)}, u32[]{:S(2)}) copy-start(s32[256]{0:T(256)} %param.14) | copy-start | bytes 3076
  0.7 0.7 %copy-start.7 = (s32[64]{0:T(128)S(1)}, s32[64]{0:T(128)}, u32[]{:S(2)}) copy-start(s32[64]{0:T(128)} %param.12) | copy-start | bytes 772
  1.3 1.2 %copy-start = (bf16[8,256,256]{2,1,0:T(8,128)(2,1)S(1)}, bf16[8,256,256]{2,1,0:T(8,128)(2,1)}, u32[]{:S(2)}) copy-start(bf16[8,256,256]{2,1,0:T(8,128)(2,1)} %pot_ref.1) | copy-start | bytes 3145732
  2.6 1.0 %copy-start.1 = (bf16[16,64,256]{2,1,0:T(8,128)(2,1)S(1)}, bf16[16,64,256]{2,1,0:T(8,128)(2,1)}, u32[]{:S(2)}) copy-start(bf16[16,64,256]{2,1,0:T(8,128)(2,1)} %res_ref.1) | copy-start | bytes 1572868
  3.6 0.9 %copy-start.2 = (bf16[256,144]{1,0:T(8,128)(2,1)S(1)}, bf16[256,144]{1,0:T(8,128)(2,1)}, u32[]{:S(2)}) copy-start(bf16[256,144]{1,0:T(8,128)(2,1)} %constant.8.clone.disc_t_ref) | copy-start | bytes 221188
  4.5 0.9 %copy-start.3 = (bf16[256,256]{1,0:T(8,128)(2,1)S(1)}, bf16[256,256]{1,0:T(8,128)(2,1)}, u32[]{:S(2)}) copy-start(bf16[256,256]{1,0:T(8,128)(2,1)} %constant.6.clone.table_ref) | copy-start | bytes 393220
  5.4 0.9 %copy-start.4 = (bf16[144,256]{1,0:T(8,128)(2,1)S(1)}, bf16[144,256]{1,0:T(8,128)(2,1)}, u32[]{:S(2)}) copy-start(bf16[144,256]{1,0:T(8,128)(2,1)} %constant.7.clone.disc_ref) | copy-start | bytes 221188
  6.3 0.8 %copy-start.5 = (bf16[1,64,256]{2,1,0:T(8,128)(2,1)S(1)}, bf16[1,64,256]{2,1,0:T(8,128)(2,1)}, u32[]{:S(2)}) copy-start(bf16[1,64,256]{2,1,0:T(8,128)(2,1)} %param.9) | copy-start | bytes 98308

commit v2 on v1

v2 whole, which is shorter than its diff:
```python
import functools

import jax
import jax.numpy as jnp
import numpy as np
from jax import lax
from jax.experimental import pallas as pl
from jax.experimental.pallas import tpu as pltpu
from jax.sharding import PartitionSpec as P

MESH = pl.DeviceIdType.MESH
GRID = 256
RADIUS = 64
ROWS = 144
TILE = 256
F32 = jnp.float32
BF16 = jnp.bfloat16
EXACT = lax.Precision.HIGHEST
UNROLL = 2
VMEM_BYTES = 60 * 2**20


def hartley_tables():
    k = np.arange(GRID)
    angle = (k[:, None] * k[None, :] % GRID).astype(np.float32) * np.float32(2.0 * np.pi / GRID)
    table = ((np.cos(angle) + np.sin(angle)) * np.float32(1.0 / np.sqrt(GRID))).astype(BF16)
    disc = np.zeros((ROWS, GRID), BF16)
    disc[: 2 * RADIUS + 1] = table[np.arange(-RADIUS, RADIUS + 1) % GRID]
    return table, disc, np.ascontiguousarray(disc.T)


def iota(shape, axis):
    return lax.broadcasted_iota(jnp.int32, shape, axis)


def dot(a, b, ca, cb, precision=None):
    return lax.dot_general(
        a, b, (((ca,), (cb,)), ((), ())), precision=precision, preferred_element_type=F32
    )


def kernel(
    n_band,
    n_ga,
    psi_ref,
    pot_ref,
    res_ref,
    cols_ref,
    counts_ref,
    order_ref,
    table_ref,
    disc_ref,
    disc_t_ref,
    applied_ref,
    inter_ref,
    cols_v,
    counts_v,
    order_v,
    psi_v,
    pot_v,
    res_v,
    table_v,
    disc_v,
    disc_t_v,
    out_v,
    ztab_v,
    cols_send,
    cols_recv,
    z_send,
    z_recv,
    pick_send,
    pick_recv,
    onehot_x,
    table_y,
    half_acc,
    half_v,
    back_v,
    packed_res,
    gather,
    red_send,
    red_recv,
    load_sem,
    send_sem,
    cols_sem,
    z_sem,
    pick_sem,
    gather_sem,
    red_sem,
    out_sem,
):
    me_b, me_g = lax.axis_index("band"), lax.axis_index("ga")
    sticks, planes, n_res = psi_ref.shape[0], pot_ref.shape[0], res_ref.shape[0]
    per_tile = TILE // sticks
    tiles = n_ga // per_tile
    me_t = me_g // per_tile
    core, column = me_b % 2, me_b // 2
    n_col = n_band // 2
    parity = lax.rem(me_g, 2)

    barrier = pltpu.get_barrier_semaphore()

    @pl.loop(1, n_ga)
    def _(d):
        to = lax.rem(me_g + d, n_ga)
        pl.semaphore_signal(barrier, inc=1, device_id={"ga": to}, device_id_type=MESH)

    @pl.loop(1, n_col)
    def _(d):
        to = lax.rem(column + d, n_col) * 2 + core
        pl.semaphore_signal(barrier, inc=1, device_id={"band": to}, device_id_type=MESH)

    other = column * 2 + 1 - core
    pl.semaphore_signal(barrier, inc=1, device_id={"band": other}, device_id_type=MESH)

    loads = [
        pltpu.make_async_copy(src, dst, load_sem.at[i])
        for i, (src, dst) in enumerate(
            (
                (cols_ref, cols_v),
                (counts_ref, counts_v),
                (order_ref, order_v),
                (psi_ref, psi_v),
                (table_ref, table_v),
                (disc_ref, disc_v),
                (disc_t_ref, disc_t_v),
                (pot_ref, pot_v),
                (res_ref, res_v),
            )
        )
    ]
    for load in loads:
        load.start()
    taken = set()

    def take(*which):
        for i in which:
            loads[i].wait()
            taken.add(i)

    def send(src, dst, phase, sem, **to):
        pltpu.make_async_remote_copy(
            src_ref=src,
            dst_ref=dst,
            send_sem=send_sem.at[phase],
            recv_sem=sem,
            device_id=to,
            device_id_type=MESH,
        ).start()

    def wait_bytes(ref, sem):
        pltpu.make_async_copy(ref, ref, sem).wait()

    def tile_at(step):
        ahead = jnp.where(step % 2 == 1, (step + 1) // 2, tiles - step // 2)
        return lax.rem(me_t + ahead, tiles)

    take(0, 1, 2)
    counts = jnp.where(
        iota((sticks, sticks), 0) == iota((sticks, sticks), 1), counts_v[...].astype(F32), 0.0
    ).sum(axis=1, keepdims=True)
    k = iota((sticks, GRID), 1)
    freq = jnp.where(k < GRID // 2, k, GRID - k)
    sphere = (2 * freq + 1).astype(F32) <= counts

    lane_half = iota((1, 2 * sticks), 1) // sticks
    own_half = lane_half == parity
    cols = cols_v[...]
    cols_send[...] = jnp.where(own_half, jnp.concatenate([cols, cols], axis=1), 0)
    pltpu.make_async_copy(cols_send, cols_recv.at[me_g], cols_sem.at[me_t]).start()

    take(3, 4)
    order_pick = (iota((GRID, n_ga * planes), 0) == order_v[...]).astype(F32).astype(BF16)
    ztab = dot(order_pick, table_v[...], 0, 0).astype(BF16)
    ztab_v[...] = ztab
    masked = jnp.where(sphere, psi_v[...].astype(F32), 0.0)
    two = jnp.concatenate(
        [jnp.where(parity == 0, masked, 0.0), jnp.where(parity == 1, masked, 0.0)], axis=0
    ).astype(BF16)
    zreal = dot(ztab, two, 1, 1).astype(BF16).astype(F32)
    z_send[...] = zreal.reshape(n_ga, planes, 2 * sticks)
    pltpu.make_async_copy(z_send.at[me_g], z_recv.at[me_g], z_sem.at[me_t]).start()
    half_acc[...] = jnp.zeros_like(half_acc)

    pl.semaphore_wait(barrier, n_ga - 1 + n_col)

    @pl.loop(1, n_ga)
    def _(d):
        to = lax.rem(me_g + n_ga // 2 + d, n_ga)
        to = jnp.where(to == me_g, lax.rem(me_g + n_ga // 2, n_ga), to)
        send(cols_send, cols_recv.at[me_g], 0, cols_sem.at[me_t], ga=to)
        send(z_send.at[to], z_recv.at[me_g], 1, z_sem.at[me_t], ga=to)

    @pl.loop(0, tiles)
    def _(step):
        t = tile_at(step)
        base = per_tile * t
        wait_bytes(cols_recv.at[pl.ds(base, per_tile)], cols_sem.at[t])
        col = jnp.concatenate(
            [cols_recv[base + i] + cols_recv[base + i + 1] for i in range(0, per_tile, 2)], axis=1
        )
        kx, ky = lax.shift_right_logical(col, 8), col & (GRID - 1)
        row = jnp.where(kx < GRID // 2, kx + RADIUS, kx + RADIUS - GRID)
        onehot_x[t] = (iota((ROWS, TILE), 0) == row).astype(F32).astype(BF16)
        onehot_y = (iota((GRID, TILE), 0) == ky).astype(F32).astype(BF16)
        table_y[t] = dot(table_v[...], onehot_y, 1, 0).astype(BF16)
        wait_bytes(z_recv.at[pl.ds(base, per_tile)], z_sem.at[t])
        z = jnp.concatenate(
            [z_recv[base + i] + z_recv[base + i + 1] for i in range(0, per_tile, 2)], axis=1
        )
        pick = onehot_x[t].reshape(ROWS // 16, 16, TILE)
        spread = jnp.concatenate(
            [
                (pick * jnp.broadcast_to(z[p : p + 1], (16, TILE)).astype(BF16)[None]).reshape(
                    ROWS, TILE
                )
                for p in range(planes)
            ],
            axis=0,
        )
        half_acc[...] += dot(spread, table_y[t], 1, 1)

    half_v[...] = half_acc[...].astype(BF16).reshape(planes, ROWS, GRID)
    take(5, 6, 7)

    @pl.loop(0, planes, unroll=UNROLL)
    def _(p):
        field = dot(disc_t_v[...], half_v[p], 1, 0)
        weighted = (pot_v[p].astype(F32) * field).astype(BF16)
        back_v[p] = dot(disc_v[...], weighted, 1, 0).astype(BF16)

    @pl.loop(0, tiles)
    def _(step):
        t = tile_at(tiles - 1 - step)
        spectrum = dot(back_v[...].reshape(planes * ROWS, GRID), table_y[t], 1, 0)
        picked = (spectrum.reshape(planes, ROWS, TILE) * onehot_x[t].astype(F32)[None]).sum(axis=1)
        picked = picked.astype(BF16).astype(F32)
        for i in range(per_tile // 2):
            pair = per_tile // 2 * t + i
            pick_send[pair] = picked[:, 2 * sticks * i : 2 * sticks * (i + 1)]
        for i in range(per_tile):
            to = per_tile * t + i

            @pl.when(to != me_g)
            def _():
                send(pick_send.at[to // 2], pick_recv.at[me_g], 2, pick_sem.at[0], ga=to)

    pltpu.make_async_copy(pick_send.at[me_g // 2], pick_recv.at[me_g], pick_sem.at[0]).start()

    def packed(low, high):
        lane = iota(low.shape, low.ndim - 1)
        spare = (lane == RADIUS) & (counts < 2 * RADIUS + 1)
        return jnp.where(
            lane < RADIUS, low, jnp.where(spare, pltpu.roll(low, 1, low.ndim - 2), high)
        )

    take(8)

    @pl.loop(0, n_res)
    def _(r):
        rows = res_v[r].astype(F32)
        packed_res[r] = packed(rows[:, : GRID // 2], rows[:, GRID // 2 :]).astype(BF16)

    wait_bytes(pick_recv, pick_sem.at[0])
    returned = jnp.where(own_half, pick_recv[...].reshape(n_ga * planes, 2 * sticks), 0.0)
    result = dot(returned.astype(BF16), ztab_v[...], 0, 0)
    result = jnp.where(sphere, result[:sticks] + result[sticks:], 0.0)
    gather[core, column] = packed(result[:, : GRID // 2], result[:, GRID // 2 :]).astype(BF16)

    for dz in range(min(2, n_col) - 1, -1, -1):
        for dx in [i for i in (2, 1, 3, 0) if i < n_col // 2 or i == 0]:
            if dx == 0 and dz == 0:
                continue
            q = column_of(column, n_col, dx, dz)
            slot = gather.at[core, column]
            send(slot, slot, 3, gather_sem.at[0, 2 * dx + dz], band=2 * q + core)
    slot = gather.at[core, column]
    send(slot, slot, 3, gather_sem.at[1, 0], band=other)
    out_v[...] = result.astype(BF16)
    store = pltpu.make_async_copy(out_v, applied_ref, out_sem.at[0])
    store.start()
    offsets = [
        (dx, dz)
        for dx, dz in ((1, 0), (3, 0), (0, 1), (2, 0), (1, 1), (3, 1), (2, 1))
        if (dx < n_col // 2 or dx == 0) and dz < n_col
    ]
    for dx, dz in offsets:
        q = column_of(column, n_col, -dx, dz)
        slot = gather.at[core, q]
        wait_bytes(slot, gather_sem.at[0, 2 * dx + dz])
        send(slot, slot, 3, gather_sem.at[1, 2 * dx + dz], band=other)

    def products(which):
        prod = jnp.zeros((n_res * 16, n_col * 16), F32)
        for g in range(sticks // 16):
            left = packed_res[:, 16 * g : 16 * g + 16, :].reshape(n_res * 16, GRID // 2)
            right = gather[which, :, 16 * g : 16 * g + 16, :].reshape(n_col * 16, GRID // 2)
            prod += dot(left, right, 1, 1)
        same = iota(prod.shape, 0) % 16 == iota(prod.shape, 1) % 16
        summed = jnp.where(same, prod, 0.0).reshape(n_res, 16, n_col * 16).sum(axis=1)
        band = iota((n_col * 16, 128), 0) // 16 * 2 + which
        fold = (band == iota((n_col * 16, 128), 1) % 16).astype(F32)
        return dot(summed, fold, 1, 0, EXACT)

    part = products(core)
    for dx, dz in [(0, 0)] + offsets:
        q = column_of(column, n_col, -dx, dz)
        wait_bytes(gather.at[1 - core, q], gather_sem.at[1, 2 * dx + dz])
    part += products(1 - core)
    part = jnp.where(iota(part.shape, 1) // 16 == iota(part.shape, 0) % 8, part, 0.0)
    red_send[...] = part.reshape(n_res // 8, 8, 128).sum(axis=1)
    pltpu.make_async_copy(red_send, red_recv.at[me_g], red_sem.at[0]).start()

    @pl.loop(1, n_ga)
    def _(d):
        to = lax.rem(me_g + d, n_ga)
        send(red_send, red_recv.at[me_g], 4, red_sem.at[0], ga=to)

    wait_bytes(red_recv, red_sem.at[0])
    inter_ref[...] = red_recv[...].sum(axis=0)

    store.wait()
    wait_bytes(cols_recv.at[pl.ds(0, n_ga - 1)], send_sem.at[0])
    wait_bytes(z_recv.at[pl.ds(0, n_ga - 1)], send_sem.at[1])
    wait_bytes(pick_recv.at[pl.ds(0, n_ga - 1)], send_sem.at[2])
    for _ in range(2):
        wait_bytes(gather.at[0, pl.ds(0, n_col - 1)], send_sem.at[3])
    wait_bytes(gather.at[0, 0], send_sem.at[3])
    wait_bytes(red_recv.at[pl.ds(0, n_ga - 1)], send_sem.at[4])


def column_of(column, n_col, dx, dz):
    if n_col == 1:
        return column
    n_x = n_col // 2
    x = lax.rem(column // 2 + dx + n_x, n_x)
    z = lax.rem(column % 2 + dz, 2)
    return 2 * x + z


def body(n_band, n_ga, psi_block, potential, resident, stick_cols, stick_counts, plane_order):
    sticks, planes, n_res = psi_block.shape[1], potential.shape[0], resident.shape[0]
    tiles = n_ga * sticks // TILE
    table, disc, disc_t = hartley_tables()
    hbm = pl.BlockSpec(memory_space=pltpu.HBM)
    vmem = pl.BlockSpec(memory_space=pltpu.VMEM)
    applied, inter = pl.pallas_call(
        functools.partial(kernel, n_band, n_ga),
        out_shape=(
            jax.ShapeDtypeStruct((sticks, GRID), BF16),
            jax.ShapeDtypeStruct((n_res // 8, 128), F32),
        ),
        in_specs=[hbm] * 9,
        out_specs=(hbm, vmem),
        scratch_shapes=[
            pltpu.VMEM((1, sticks), jnp.int32),
            pltpu.VMEM((1, sticks), jnp.int32),
            pltpu.VMEM((1, n_ga * planes), jnp.int32),
            pltpu.VMEM((sticks, GRID), BF16),
            pltpu.VMEM(potential.shape, BF16),
            pltpu.VMEM(resident.shape, BF16),
            pltpu.VMEM(table.shape, BF16),
            pltpu.VMEM(disc.shape, BF16),
            pltpu.VMEM(disc_t.shape, BF16),
            pltpu.VMEM((sticks, GRID), BF16),
            pltpu.VMEM((n_ga * planes, GRID), BF16),
            pltpu.VMEM((1, 2 * sticks), jnp.int32),
            pltpu.VMEM((n_ga, 1, 2 * sticks), jnp.int32),
            pltpu.VMEM((n_ga, planes, 2 * sticks), F32),
            pltpu.VMEM((n_ga, planes, 2 * sticks), F32),
            pltpu.VMEM((n_ga // 2, planes, 2 * sticks), F32),
            pltpu.VMEM((n_ga, planes, 2 * sticks), F32),
            pltpu.VMEM((tiles, ROWS, TILE), BF16),
            pltpu.VMEM((tiles, GRID, TILE), BF16),
            pltpu.VMEM((planes * ROWS, GRID), F32),
            pltpu.VMEM((planes, ROWS, GRID), BF16),
            pltpu.VMEM((planes, ROWS, GRID), BF16),
            pltpu.VMEM((n_res, sticks, GRID // 2), BF16),
            pltpu.VMEM((2, n_band // 2, sticks, GRID // 2), BF16),
            pltpu.VMEM((n_res // 8, 128), F32),
            pltpu.VMEM((n_ga, n_res // 8, 128), F32),
            pltpu.SemaphoreType.DMA((9,)),
            pltpu.SemaphoreType.DMA((5,)),
            pltpu.SemaphoreType.DMA((tiles,)),
            pltpu.SemaphoreType.DMA((tiles,)),
            pltpu.SemaphoreType.DMA((1,)),
            pltpu.SemaphoreType.DMA((2, 8)),
            pltpu.SemaphoreType.DMA((1,)),
            pltpu.SemaphoreType.DMA((1,)),
        ],
        compiler_params=pltpu.CompilerParams(
            collective_id=0, has_side_effects=True, vmem_limit_bytes=VMEM_BYTES
        ),
    )(
        psi_block[0],
        potential,
        resident,
        stick_cols[None],
        stick_counts[None],
        plane_order[None],
        table,
        disc,
        disc_t,
    )
    return applied[None], inter.reshape(n_res, 16)[:, :n_band]


def solution(mesh):
    in_specs = (
        P("band", "ga", None),
        P("ga", None, None),
        P("band", "ga", None),
        P("ga"),
        P("ga"),
        P(),
    )
    out_specs = (P("band", "ga", None), P("band", None))
    step = functools.partial(body, mesh.shape["band"], mesh.shape["ga"])
    return jax.shard_map(step, mesh=mesh, in_specs=in_specs, out_specs=out_specs, check_vma=False)
```

time: 66 us -> 53.9 us (0.82)
  Pallas kernels: 57.3 us -> 50.4 us
  local copies, waits for them, and re-layouts: 7.68 us -> 2.68 us
    pallas_call x1, Pallas kernels: 57.3 us -> 50.4 us  [body(): pl.pallas_call(functools.partial(kernel, n_band, n_ga), out_shape=(jax.Sh...]
    unnamed x19 -> x3, local copies, waits for them, and re-layouts: 7 us -> 2 us
where the time goes in v2:
time: 53.9 us; the launch traced here: 53.7 us
  Pallas kernels  50.4 us (94%)
  local copies, waits for them, and re-layouts  2.68 us (5%)
  between operations  0.65 us (1%)
    pallas_call x1, Pallas kernels, body(): pl.pallas_call(functools.partial(kernel, n_band, n_ga), out_shape=(jax.Sh...  50.4 us
    unnamed x3, local copies, waits for them, and re-layouts  2 us

profile of v2, /device:TPU:1, one launch (start us, length us, event | category | flops | bytes accessed | tf_op | source)
XLA Modules:
  0.0 53.7 jit_solution(5618140819528817268)
XLA Ops:
  0.6 50.4 %shard_map.104 = (bf16[64,256]{1,0:T(8,128)(2,1)}, f32[2,128]{1,0:T(2,128)}) custom-call(bf16[64,256]{1,0:T(8,128)(2,1)} %bitcast.5, bf16[8,256,256]{2,1,0:T(8,128)(2,1)} %pot_ref.1, bf16[16,64,256]{2,1,0:T(8,128)(2,1)} %res_ref.1, s32[1,64]{1,0:T(1,128)} %bitcast.8, s32[1,64]{1,0:T(1,128)} %bitcast.9, s32[1,256]{1,0:T(1,128)} %bitcast.7, ...), custom_call_target="tpu_custom_call" | custom-call | tf_op jit(solution)/shard_map/pallas_call | solution.py:346
  51.0 0.0 copy-start
  51.0 0.6 %copy-done = f32[2,128]{1,0:T(2,128)S(1)} copy-done((f32[2,128]{1,0:T(2,128)S(1)}, f32[2,128]{1,0:T(2,128)}, u32[]{:S(2)}) %copy-start) | copy-done | bytes 1048
  51.6 0.7 %reshape.7 = f32[16,16]{1,0:T(8,128)} reshape(f32[2,128]{1,0:T(2,128)S(1)} %copy-done) | data formatting | bytes 2048 | tf_op jit(solution)/shard_map/reshape | solution.py:404
  52.3 1.4 %copy.12 = bf16[1,64,256]{2,1,0:T(8,128)(2,1)} copy(bf16[1,64,256]{2,1,0:T(8,128)(2,1)} %bitcast.6) | data formatting | bytes 65536
Async XLA Ops:
  51.0 0.6 %copy-start = (f32[2,128]{1,0:T(2,128)S(1)}, f32[2,128]{1,0:T(2,128)}, u32[]{:S(2)}) copy-start(f32[2,128]{1,0:T(2,128)} %get-tuple-element.5) | copy-start | bytes 3076

commit v3 on v2

--- a/solution.py
+++ b/solution.py
@@ -16,7 +16,7 @@
 F32 = jnp.float32
 BF16 = jnp.bfloat16
 EXACT = lax.Precision.HIGHEST
-UNROLL = 2
+UNROLL = 4
 VMEM_BYTES = 60 * 2**20
 
 
@@ -52,7 +52,7 @@
     disc_ref,
     disc_t_ref,
     applied_ref,
-    inter_ref,
+    red_recv,
     cols_v,
     counts_v,
     order_v,
@@ -78,7 +78,6 @@
     packed_res,
     gather,
     red_send,
-    red_recv,
     load_sem,
     send_sem,
     cols_sem,
@@ -150,6 +149,15 @@
     def wait_bytes(ref, sem):
         pltpu.make_async_copy(ref, ref, sem).wait()
 
+    def swap(even, odd):
+        low = iota(even.shape, 1) < sticks
+        lower = jnp.where(low, even, pltpu.roll(odd, sticks, 1))
+        upper = jnp.where(low, pltpu.roll(even, sticks, 1), odd)
+        return jnp.concatenate([lower, upper], axis=0)
+
+    def z_pair(i):
+        return z_recv[i], z_recv[i + 1]
+
     def tile_at(step):
         ahead = jnp.where(step % 2 == 1, (step + 1) // 2, tiles - step // 2)
         return lax.rem(me_t + ahead, tiles)
@@ -169,15 +177,19 @@
     pltpu.make_async_copy(cols_send, cols_recv.at[me_g], cols_sem.at[me_t]).start()
 
     take(3, 4)
-    order_pick = (iota((GRID, n_ga * planes), 0) == order_v[...]).astype(F32).astype(BF16)
+    n_planes, half = n_ga * planes, planes // 2
+    q = iota((n_planes, n_planes), 1)
+    moved = q % (n_planes // 2) // half * planes + q // (n_planes // 2) * half + q % half
+    move = (iota((n_planes, n_planes), 0) == moved).astype(F32).astype(BF16)
+    order = jnp.broadcast_to(order_v[...].astype(F32).astype(BF16), (16, n_planes))
+    order = dot(order, move, 1, 0)[:1].astype(jnp.int32)
+    order_pick = (iota((GRID, n_planes), 0) == order).astype(F32).astype(BF16)
     ztab = dot(order_pick, table_v[...], 0, 0).astype(BF16)
     ztab_v[...] = ztab
-    masked = jnp.where(sphere, psi_v[...].astype(F32), 0.0)
-    two = jnp.concatenate(
-        [jnp.where(parity == 0, masked, 0.0), jnp.where(parity == 1, masked, 0.0)], axis=0
-    ).astype(BF16)
-    zreal = dot(ztab, two, 1, 1).astype(BF16).astype(F32)
-    z_send[...] = zreal.reshape(n_ga, planes, 2 * sticks)
+    masked = jnp.where(sphere, psi_v[...].astype(F32), 0.0).astype(BF16)
+    zreal = dot(ztab, masked, 1, 1).astype(BF16).astype(F32)
+    zreal = jnp.concatenate([zreal[: n_planes // 2], zreal[n_planes // 2 :]], axis=1)
+    z_send[...] = zreal.reshape(n_ga, half, 2 * sticks)
     pltpu.make_async_copy(z_send.at[me_g], z_recv.at[me_g], z_sem.at[me_t]).start()
     half_acc[...] = jnp.zeros_like(half_acc)
 
@@ -204,9 +216,7 @@
         onehot_y = (iota((GRID, TILE), 0) == ky).astype(F32).astype(BF16)
         table_y[t] = dot(table_v[...], onehot_y, 1, 0).astype(BF16)
         wait_bytes(z_recv.at[pl.ds(base, per_tile)], z_sem.at[t])
-        z = jnp.concatenate(
-            [z_recv[base + i] + z_recv[base + i + 1] for i in range(0, per_tile, 2)], axis=1
-        )
+        z = jnp.concatenate([swap(*z_pair(base + i)) for i in range(0, per_tile, 2)], axis=1)
         pick = onehot_x[t].reshape(ROWS // 16, 16, TILE)
         spread = jnp.concatenate(
             [
@@ -236,15 +246,19 @@
         picked = picked.astype(BF16).astype(F32)
         for i in range(per_tile // 2):
             pair = per_tile // 2 * t + i
-            pick_send[pair] = picked[:, 2 * sticks * i : 2 * sticks * (i + 1)]
+            rows = picked[:, 2 * sticks * i : 2 * sticks * (i + 1)]
+            low = iota((half, 2 * sticks), 1) < sticks
+            lower, upper = rows[:half], rows[half:]
+            pick_send[2 * pair] = jnp.where(low, lower, pltpu.roll(upper, sticks, 1))
+            pick_send[2 * pair + 1] = jnp.where(low, pltpu.roll(lower, sticks, 1), upper)
         for i in range(per_tile):
             to = per_tile * t + i
 
             @pl.when(to != me_g)
             def _():
-                send(pick_send.at[to // 2], pick_recv.at[me_g], 2, pick_sem.at[0], ga=to)
-
-    pltpu.make_async_copy(pick_send.at[me_g // 2], pick_recv.at[me_g], pick_sem.at[0]).start()
+                send(pick_send.at[to], pick_recv.at[me_g], 2, pick_sem.at[0], ga=to)
+
+    pltpu.make_async_copy(pick_send.at[me_g], pick_recv.at[me_g], pick_sem.at[0]).start()
 
     def packed(low, high):
         lane = iota(low.shape, low.ndim - 1)
@@ -261,9 +275,10 @@
         packed_res[r] = packed(rows[:, : GRID // 2], rows[:, GRID // 2 :]).astype(BF16)
 
     wait_bytes(pick_recv, pick_sem.at[0])
-    returned = jnp.where(own_half, pick_recv[...].reshape(n_ga * planes, 2 * sticks), 0.0)
+    returned = pick_recv[...].reshape(n_planes // 2, 2 * sticks)
+    returned = jnp.concatenate([returned[:, :sticks], returned[:, sticks:]], axis=0)
     result = dot(returned.astype(BF16), ztab_v[...], 0, 0)
-    result = jnp.where(sphere, result[:sticks] + result[sticks:], 0.0)
+    result = jnp.where(sphere, result, 0.0)
     gather[core, column] = packed(result[:, : GRID // 2], result[:, GRID // 2 :]).astype(BF16)
 
     for dz in range(min(2, n_col) - 1, -1, -1):
@@ -316,8 +331,6 @@
         send(red_send, red_recv.at[me_g], 4, red_sem.at[0], ga=to)
 
     wait_bytes(red_recv, red_sem.at[0])
-    inter_ref[...] = red_recv[...].sum(axis=0)
-
     store.wait()
     wait_bytes(cols_recv.at[pl.ds(0, n_ga - 1)], send_sem.at[0])
     wait_bytes(z_recv.at[pl.ds(0, n_ga - 1)], send_sem.at[1])
@@ -335,6 +348,16 @@
     x = lax.rem(column // 2 + dx + n_x, n_x)
     z = lax.rem(column % 2 + dz, 2)
     return 2 * x + z
+
+
+def finish(applied_ref, parts_ref, applied_out, inter_out):
+    applied_out[0] = applied_ref[...]
+    n_res = inter_out.shape[0]
+    total = parts_ref[...].sum(axis=0)
+    total = jnp.broadcast_to(total[:, None, :], (n_res // 8, 8, 128)).reshape(n_res, 128)
+    total = jnp.where(iota(total.shape, 1) // 16 == iota(total.shape, 0) % 8, total, 0.0)
+    fold = (iota((128, 16), 0) % 16 == iota((128, 16), 1)).astype(F32)
+    inter_out[...] = dot(total, fold, 1, 0, EXACT)
 
 
 def body(n_band, n_ga, psi_block, potential, resident, stick_cols, stick_counts, plane_order):
@@ -347,10 +370,10 @@
         functools.partial(kernel, n_band, n_ga),
         out_shape=(
             jax.ShapeDtypeStruct((sticks, GRID), BF16),
-            jax.ShapeDtypeStruct((n_res // 8, 128), F32),
+            jax.ShapeDtypeStruct((n_ga, n_res // 8, 128), F32),
         ),
         in_specs=[hbm] * 9,
-        out_specs=(hbm, vmem),
+        out_specs=(hbm, hbm),
         scratch_shapes=[
             pltpu.VMEM((1, sticks), jnp.int32),
             pltpu.VMEM((1, sticks), jnp.int32),
@@ -365,10 +388,10 @@
             pltpu.VMEM((n_ga * planes, GRID), BF16),
             pltpu.VMEM((1, 2 * sticks), jnp.int32),
             pltpu.VMEM((n_ga, 1, 2 * sticks), jnp.int32),
-            pltpu.VMEM((n_ga, planes, 2 * sticks), F32),
-            pltpu.VMEM((n_ga, planes, 2 * sticks), F32),
-            pltpu.VMEM((n_ga // 2, planes, 2 * sticks), F32),
-            pltpu.VMEM((n_ga, planes, 2 * sticks), F32),
+            pltpu.VMEM((n_ga, planes // 2, 2 * sticks), F32),
+            pltpu.VMEM((n_ga, planes // 2, 2 * sticks), F32),
+            pltpu.VMEM((n_ga, planes // 2, 2 * sticks), F32),
+            pltpu.VMEM((n_ga, planes // 2, 2 * sticks), F32),
             pltpu.VMEM((tiles, ROWS, TILE), BF16),
             pltpu.VMEM((tiles, GRID, TILE), BF16),
             pltpu.VMEM((planes * ROWS, GRID), F32),
@@ -377,7 +400,6 @@
             pltpu.VMEM((n_res, sticks, GRID // 2), BF16),
             pltpu.VMEM((2, n_band // 2, sticks, GRID // 2), BF16),
             pltpu.VMEM((n_res // 8, 128), F32),
-            pltpu.VMEM((n_ga, n_res // 8, 128), F32),
             pltpu.SemaphoreType.DMA((9,)),
             pltpu.SemaphoreType.DMA((5,)),
             pltpu.SemaphoreType.DMA((tiles,)),
@@ -401,7 +423,16 @@
         disc,
         disc_t,
     )
-    return applied[None], inter.reshape(n_res, 16)[:, :n_band]
+    applied, inter = pl.pallas_call(
+        finish,
+        out_shape=(
+            jax.ShapeDtypeStruct((1, sticks, GRID), BF16),
+            jax.ShapeDtypeStruct((n_res, 16), F32),
+        ),
+        in_specs=[vmem] * 2,
+        out_specs=(vmem, vmem),
+    )(applied, inter)
+    return applied, inter[:, :n_band]
 
 
 def solution(mesh):

time: 53.9 us -> 50.8 us (0.942)
  local copies, waits for them, and re-layouts: 2.68 us -> 0 us
    pallas_call x1, Pallas kernels: 50.4 us -> 48.3 us  [body(): pl.pallas_call(functools.partial(kernel, n_band, n_ga), out_shape=(jax.Sh...]
    unnamed x3 -> x0, local copies, waits for them, and re-layouts: 2 us -> none
    pallas_call x0 -> x1, Pallas kernels: none -> 1.57 us  [body(): pl.pallas_call(finish, out_shape=(jax.ShapeDtypeStruct((1, sticks, GRID),...]
    reshape x1 -> x0, local copies, waits for them, and re-layouts: 0.68 us -> none  [body(): return (applied[None], inter.reshape(n_res, 16)[:, :n_band])]
where the time goes in v3:
time: 50.8 us; the launch traced here: 50.6 us
  Pallas kernels  49.9 us (98%)
  between operations  0.64 us (1%)
    pallas_call x1, Pallas kernels, body(): pl.pallas_call(functools.partial(kernel, n_band, n_ga), out_shape=(jax.Sh...  48.3 us
    pallas_call x1, Pallas kernels, body(): pl.pallas_call(finish, out_shape=(jax.ShapeDtypeStruct((1, sticks, GRID),...  1.57 us

profile of v3, /device:TPU:1, one launch (start us, length us, event | category | flops | bytes accessed | tf_op | source)
XLA Modules:
  0.0 50.6 jit_solution(12713431899863711631)
XLA Ops:
  0.6 48.3 %shard_map.104 = (bf16[64,256]{1,0:T(8,128)(2,1)}, f32[32,2,128]{2,1,0:T(2,128)}) custom-call(bf16[64,256]{1,0:T(8,128)(2,1)} %bitcast.4, bf16[8,256,256]{2,1,0:T(8,128)(2,1)} %pot_ref.1, bf16[16,64,256]{2,1,0:T(8,128)(2,1)} %res_ref.1, s32[1,64]{1,0:T(1,128)} %bitcast.6, s32[1,64]{1,0:T(1,128)} %bitcast.7, s32[1,256]{1,0:T(1,128)} %bitcast.5, ...), custom_call_target="tpu_custom_call" | custom-call | tf_op jit(solution)/shard_map/pallas_call | solution.py:369
  49.0 1.6 %shard_map.105 = (bf16[1,64,256]{2,1,0:T(8,128)(2,1)}, f32[16,16]{1,0:T(8,128)}) custom-call(bf16[64,256]{1,0:T(8,128)(2,1)} %get-tuple-element.4.applied_ref, f32[32,2,128]{2,1,0:T(2,128)} %get-tuple-element.5.parts_ref), custom_call_target="tpu_custom_call" | custom-call | tf_op jit(solution)/shard_map/pallas_call | solution.py:426

commit v4 on v3

--- a/solution.py
+++ b/solution.py
@@ -73,7 +73,6 @@
     onehot_x,
     table_y,
     half_acc,
-    half_v,
     back_v,
     packed_res,
     gather,
@@ -227,16 +226,18 @@
             ],
             axis=0,
         )
-        half_acc[...] += dot(spread, table_y[t], 1, 1)
-
-    half_v[...] = half_acc[...].astype(BF16).reshape(planes, ROWS, GRID)
+        half_acc[...] += dot(spread, table_y[t], 1, 1).reshape(planes, ROWS, GRID)
+
     take(5, 6, 7)
 
     @pl.loop(0, planes, unroll=UNROLL)
     def _(p):
-        field = dot(disc_t_v[...], half_v[p], 1, 0)
-        weighted = (pot_v[p].astype(F32) * field).astype(BF16)
-        back_v[p] = dot(disc_v[...], weighted, 1, 0).astype(BF16)
+        field = dot(disc_t_v[...], half_acc[p].astype(BF16), 1, 0)
+        pot_v[p] = (pot_v[p].astype(F32) * field).astype(BF16)
+
+    @pl.loop(0, planes, unroll=UNROLL)
+    def _(p):
+        back_v[p] = dot(disc_v[...], pot_v[p], 1, 0).astype(BF16)
 
     @pl.loop(0, tiles)
     def _(step):
@@ -252,7 +253,7 @@
             pick_send[2 * pair] = jnp.where(low, lower, pltpu.roll(upper, sticks, 1))
             pick_send[2 * pair + 1] = jnp.where(low, pltpu.roll(lower, sticks, 1), upper)
         for i in range(per_tile):
-            to = per_tile * t + i
+            to = per_tile * t + (i + me_g) % per_tile
 
             @pl.when(to != me_g)
             def _():
@@ -394,8 +395,7 @@
             pltpu.VMEM((n_ga, planes // 2, 2 * sticks), F32),
             pltpu.VMEM((tiles, ROWS, TILE), BF16),
             pltpu.VMEM((tiles, GRID, TILE), BF16),
-            pltpu.VMEM((planes * ROWS, GRID), F32),
-            pltpu.VMEM((planes, ROWS, GRID), BF16),
+            pltpu.VMEM((planes, ROWS, GRID), F32),
             pltpu.VMEM((planes, ROWS, GRID), BF16),
             pltpu.VMEM((n_res, sticks, GRID // 2), BF16),
             pltpu.VMEM((2, n_band // 2, sticks, GRID // 2), BF16),

time: 50.8 us -> 49.8 us (0.980)
  Pallas kernels: 49.9 us -> 48.9 us
    pallas_call x1, Pallas kernels: 48.3 us -> 47.3 us  [body(): pl.pallas_call(functools.partial(kernel, n_band, n_ga), out_shape=(jax.Sh...]
where the time goes in v4:
time: 49.8 us; the launch traced here: 49.6 us
  Pallas kernels  48.9 us (98%)
  between operations  0.64 us (1%)
    pallas_call x1, Pallas kernels, body(): pl.pallas_call(functools.partial(kernel, n_band, n_ga), out_shape=(jax.Sh...  47.3 us
    pallas_call x1, Pallas kernels, body(): pl.pallas_call(finish, out_shape=(jax.ShapeDtypeStruct((1, sticks, GRID),...  1.57 us

profile of v4, /device:TPU:1, one launch (start us, length us, event | category | flops | bytes accessed | tf_op | source)
XLA Modules:
  0.0 49.6 jit_solution(15538447583254144489)
XLA Ops:
  0.6 47.3 %shard_map.104 = (bf16[64,256]{1,0:T(8,128)(2,1)}, f32[32,2,128]{2,1,0:T(2,128)}) custom-call(bf16[64,256]{1,0:T(8,128)(2,1)} %bitcast.4, bf16[8,256,256]{2,1,0:T(8,128)(2,1)} %pot_ref.1, bf16[16,64,256]{2,1,0:T(8,128)(2,1)} %res_ref.1, s32[1,64]{1,0:T(1,128)} %bitcast.6, s32[1,64]{1,0:T(1,128)} %bitcast.7, s32[1,256]{1,0:T(1,128)} %bitcast.5, ...), custom_call_target="tpu_custom_call" | custom-call | tf_op jit(solution)/shard_map/pallas_call | solution.py:370
  48.0 1.6 %shard_map.105 = (bf16[1,64,256]{2,1,0:T(8,128)(2,1)}, f32[16,16]{1,0:T(8,128)}) custom-call(bf16[64,256]{1,0:T(8,128)(2,1)} %get-tuple-element.4.applied_ref, f32[32,2,128]{2,1,0:T(2,128)} %get-tuple-element.5.parts_ref), custom_call_target="tpu_custom_call" | custom-call | tf_op jit(solution)/shard_map/pallas_call | solution.py:426

commit v5 on v4

--- a/solution.py
+++ b/solution.py
@@ -16,7 +16,7 @@
 F32 = jnp.float32
 BF16 = jnp.bfloat16
 EXACT = lax.Precision.HIGHEST
-UNROLL = 4
+UNROLL = 8
 VMEM_BYTES = 60 * 2**20
 
 
@@ -296,7 +296,7 @@
     store.start()
     offsets = [
         (dx, dz)
-        for dx, dz in ((1, 0), (3, 0), (0, 1), (2, 0), (1, 1), (3, 1), (2, 1))
+        for dx, dz in ((1, 0), (3, 0), (2, 0), (0, 1), (1, 1), (3, 1), (2, 1))
         if (dx < n_col // 2 or dx == 0) and dz < n_col
     ]
     for dx, dz in offsets:

time: 49.8 us -> 49.2 us (0.988)
  Pallas kernels: 48.9 us -> 48.4 us
    pallas_call x1, Pallas kernels: 47.3 us -> 46.8 us  [body(): pl.pallas_call(functools.partial(kernel, n_band, n_ga), out_shape=(jax.Sh...]
where the time goes in v5:
time: 49.2 us; the launch traced here: 49 us
  Pallas kernels  48.4 us (98%)
  between operations  0.64 us (1%)
    pallas_call x1, Pallas kernels, body(): pl.pallas_call(functools.partial(kernel, n_band, n_ga), out_shape=(jax.Sh...  46.8 us
    pallas_call x1, Pallas kernels, body(): pl.pallas_call(finish, out_shape=(jax.ShapeDtypeStruct((1, sticks, GRID),...  1.57 us

profile of v5, /device:TPU:1, one launch (start us, length us, event | category | flops | bytes accessed | tf_op | source)
XLA Modules:
  0.0 49.0 jit_solution(8474905296792874728)
XLA Ops:
  0.6 46.8 %shard_map.104 = (bf16[64,256]{1,0:T(8,128)(2,1)}, f32[32,2,128]{2,1,0:T(2,128)}) custom-call(bf16[64,256]{1,0:T(8,128)(2,1)} %bitcast.4, bf16[8,256,256]{2,1,0:T(8,128)(2,1)} %pot_ref.1, bf16[16,64,256]{2,1,0:T(8,128)(2,1)} %res_ref.1, s32[1,64]{1,0:T(1,128)} %bitcast.6, s32[1,64]{1,0:T(1,128)} %bitcast.7, s32[1,256]{1,0:T(1,128)} %bitcast.5, ...), custom_call_target="tpu_custom_call" | custom-call | tf_op jit(solution)/shard_map/pallas_call | solution.py:370
  47.5 1.6 %shard_map.105 = (bf16[1,64,256]{2,1,0:T(8,128)(2,1)}, f32[16,16]{1,0:T(8,128)}) custom-call(bf16[64,256]{1,0:T(8,128)(2,1)} %get-tuple-element.4.applied_ref, f32[32,2,128]{2,1,0:T(2,128)} %get-tuple-element.5.parts_ref), custom_call_target="tpu_custom_call" | custom-call | tf_op jit(solution)/shard_map/pallas_call | solution.py:426

commit v6 on v5

--- a/solution.py
+++ b/solution.py
@@ -95,6 +95,7 @@
     n_col = n_band // 2
     parity = lax.rem(me_g, 2)
 
+    far = (2, 1) if n_col == 8 else None
     barrier = pltpu.get_barrier_semaphore()
 
     @pl.loop(1, n_ga)
@@ -107,6 +108,9 @@
         to = lax.rem(column + d, n_col) * 2 + core
         pl.semaphore_signal(barrier, inc=1, device_id={"band": to}, device_id_type=MESH)
 
+    if far is not None:
+        to = 2 * column_of(column, n_col, *far) + 1 - core
+        pl.semaphore_signal(barrier, inc=1, device_id={"band": to}, device_id_type=MESH)
     other = column * 2 + 1 - core
     pl.semaphore_signal(barrier, inc=1, device_id={"band": other}, device_id_type=MESH)
 
@@ -192,7 +196,7 @@
     pltpu.make_async_copy(z_send.at[me_g], z_recv.at[me_g], z_sem.at[me_t]).start()
     half_acc[...] = jnp.zeros_like(half_acc)
 
-    pl.semaphore_wait(barrier, n_ga - 1 + n_col)
+    pl.semaphore_wait(barrier, n_ga - 1 + n_col + (far is not None))
 
     @pl.loop(1, n_ga)
     def _(d):
@@ -290,6 +294,9 @@
             slot = gather.at[core, column]
             send(slot, slot, 3, gather_sem.at[0, 2 * dx + dz], band=2 * q + core)
     slot = gather.at[core, column]
+    if far is not None:
+        q = column_of(column, n_col, *far)
+        send(slot, slot, 3, gather_sem.at[1, 2 * far[0] + far[1]], band=2 * q + 1 - core)
     send(slot, slot, 3, gather_sem.at[1, 0], band=other)
     out_v[...] = result.astype(BF16)
     store = pltpu.make_async_copy(out_v, applied_ref, out_sem.at[0])
@@ -303,7 +310,8 @@
         q = column_of(column, n_col, -dx, dz)
         slot = gather.at[core, q]
         wait_bytes(slot, gather_sem.at[0, 2 * dx + dz])
-        send(slot, slot, 3, gather_sem.at[1, 2 * dx + dz], band=other)
+        if (dx, dz) != far:
+            send(slot, slot, 3, gather_sem.at[1, 2 * dx + dz], band=other)
 
     def products(which):
         prod = jnp.zeros((n_res * 16, n_col * 16), F32)

time: 49.2 us -> 49.3 us (level)
  no operation moved by 1% of the time
where the time goes in v6:
time: 49.3 us; the launch traced here: 49.1 us
  Pallas kernels  48.5 us (98%)
  between operations  0.64 us (1%)
    pallas_call x1, Pallas kernels, body(): pl.pallas_call(functools.partial(kernel, n_band, n_ga), out_shape=(jax.Sh...  46.9 us
    pallas_call x1, Pallas kernels, body(): pl.pallas_call(finish, out_shape=(jax.ShapeDtypeStruct((1, sticks, GRID),...  1.57 us

profile of v6, /device:TPU:1, one launch (start us, length us, event | category | flops | bytes accessed | tf_op | source)
XLA Modules:
  0.0 49.1 jit_solution(6287824959055625018)
XLA Ops:
  0.6 46.9 %shard_map.104 = (bf16[64,256]{1,0:T(8,128)(2,1)}, f32[32,2,128]{2,1,0:T(2,128)}) custom-call(bf16[64,256]{1,0:T(8,128)(2,1)} %bitcast.4, bf16[8,256,256]{2,1,0:T(8,128)(2,1)} %pot_ref.1, bf16[16,64,256]{2,1,0:T(8,128)(2,1)} %res_ref.1, s32[1,64]{1,0:T(1,128)} %bitcast.6, s32[1,64]{1,0:T(1,128)} %bitcast.7, s32[1,256]{1,0:T(1,128)} %bitcast.5, ...), custom_call_target="tpu_custom_call" | custom-call | tf_op jit(solution)/shard_map/pallas_call | solution.py:378
  47.5 1.6 %shard_map.105 = (bf16[1,64,256]{2,1,0:T(8,128)(2,1)}, f32[16,16]{1,0:T(8,128)}) custom-call(bf16[64,256]{1,0:T(8,128)(2,1)} %get-tuple-element.4.applied_ref, f32[32,2,128]{2,1,0:T(2,128)} %get-tuple-element.5.parts_ref), custom_call_target="tpu_custom_call" | custom-call | tf_op jit(solution)/shard_map/pallas_call | solution.py:434

commit v7 on v5

--- a/solution.py
+++ b/solution.py
@@ -190,16 +190,19 @@
     zreal = jnp.concatenate([zreal[: n_planes // 2], zreal[n_planes // 2 :]], axis=1)
     z_send[...] = zreal.reshape(n_ga, half, 2 * sticks)
     pltpu.make_async_copy(z_send.at[me_g], z_recv.at[me_g], z_sem.at[me_t]).start()
-    half_acc[...] = jnp.zeros_like(half_acc)
 
     pl.semaphore_wait(barrier, n_ga - 1 + n_col)
 
-    @pl.loop(1, n_ga)
-    def _(d):
-        to = lax.rem(me_g + n_ga // 2 + d, n_ga)
-        to = jnp.where(to == me_g, lax.rem(me_g + n_ga // 2, n_ga), to)
+    def send_sticks(ahead):
+        to = lax.rem(me_g + ahead, n_ga)
         send(cols_send, cols_recv.at[me_g], 0, cols_sem.at[me_t], ga=to)
         send(z_send.at[to], z_recv.at[me_g], 1, z_sem.at[me_t], ga=to)
+
+    quarter = n_ga // 4
+    pl.loop(quarter, 3 * quarter + 1)(send_sticks)
+    half_acc[...] = jnp.zeros_like(half_acc)
+    pl.loop(3 * quarter + 1, n_ga)(send_sticks)
+    pl.loop(1, quarter)(send_sticks)
 
     @pl.loop(0, tiles)
     def _(step):

time: 49.2 us -> 50.1 us (1.018)
  Pallas kernels: 48.4 us -> 49.2 us
    pallas_call x1, Pallas kernels: 46.8 us -> 47.6 us  [body(): pl.pallas_call(functools.partial(kernel, n_band, n_ga), out_shape=(jax.Sh...]
where the time goes in v7:
time: 50.1 us; the launch traced here: 49.9 us
  Pallas kernels  49.2 us (98%)
  between operations  0.64 us (1%)
    pallas_call x1, Pallas kernels, body(): pl.pallas_call(functools.partial(kernel, n_band, n_ga), out_shape=(jax.Sh...  47.6 us
    pallas_call x1, Pallas kernels, body(): pl.pallas_call(finish, out_shape=(jax.ShapeDtypeStruct((1, sticks, GRID),...  1.57 us

profile of v7, /device:TPU:1, one launch (start us, length us, event | category | flops | bytes accessed | tf_op | source)
XLA Modules:
  0.0 49.9 jit_solution(6989756159192574983)
XLA Ops:
  0.6 47.6 %shard_map.104 = (bf16[64,256]{1,0:T(8,128)(2,1)}, f32[32,2,128]{2,1,0:T(2,128)}) custom-call(bf16[64,256]{1,0:T(8,128)(2,1)} %bitcast.4, bf16[8,256,256]{2,1,0:T(8,128)(2,1)} %pot_ref.1, bf16[16,64,256]{2,1,0:T(8,128)(2,1)} %res_ref.1, s32[1,64]{1,0:T(1,128)} %bitcast.6, s32[1,64]{1,0:T(1,128)} %bitcast.7, s32[1,256]{1,0:T(1,128)} %bitcast.5, ...), custom_call_target="tpu_custom_call" | custom-call | tf_op jit(solution)/shard_map/pallas_call | solution.py:373
  48.3 1.6 %shard_map.105 = (bf16[1,64,256]{2,1,0:T(8,128)(2,1)}, f32[16,16]{1,0:T(8,128)}) custom-call(bf16[64,256]{1,0:T(8,128)(2,1)} %get-tuple-element.4.applied_ref, f32[32,2,128]{2,1,0:T(2,128)} %get-tuple-element.5.parts_ref), custom_call_target="tpu_custom_call" | custom-call | tf_op jit(solution)/shard_map/pallas_call | solution.py:429
